TPU v7x, 32 devices: a whole 2x2x4 slice. The times are simulated.
32 devices in a mesh: groups: 2 (over y), expert: 16 (over z, x, core), head: 1.
Axes of the slice: x: 2, y: 2, z: 4, core: 2. Of those that a mesh axis runs over, the one named last changes fastest.
Arguments:
- sources: bfloat16 [4096, 1024], P(('groups', 'expert')), parts along dimension 0, may hold values from -6 to 6
- enc_gain: float32 [1024], replicated, may hold values from 0.1 to 1.9
- route_ids: int32 [4096, 2], P(('groups', 'expert')), parts along dimension 0, may hold values from 0 to 7, all different within a row; in each aligned block of 128 rows (0 to 127, 128 to 255, ...) at most 40 rows name the same one
- route_gates: float32 [4096, 2], P(('groups', 'expert')), parts along dimension 0, may hold values from 0.2 to 1
- w_in: bfloat16 [16, 1024, 2048], P('expert', None, 'head'), may hold values from -0.1875 to 0.1875
- w_out: bfloat16 [16, 2048, 1024], P('expert', 'head'), may hold values from -0.09375 to 0.09375
- targets: bfloat16 [4096, 1024], P(('groups', 'expert')), parts along dimension 0, may hold values from -6 to 6
- dec_gain: float32 [1024], replicated, may hold values from 0.1 to 1.9
- src_lengths: int32 [64], P(('groups', 'expert')), parts along dimension 0, may hold values from 16 to 64, as said below
- tgt_lengths: int32 [64], P(('groups', 'expert')), parts along dimension 0, may hold values from 16 to 64, as said below
- w_query: bfloat16 [1024, 1024], P('expert', 'head'), may hold values from -60 to 60
- w_key: bfloat16 [1024, 1024], P('expert', 'head'), may hold values from -0.1875 to 0.1875
- w_value: bfloat16 [1024, 1024], P('expert', 'head'), may hold values from -0.1875 to 0.1875
- w_attn: bfloat16 [1024, 1024], P('expert', 'head'), may hold values from -0.1875 to 0.1875
Outputs:
- memory: bfloat16 [4096, 1024], P(('groups', 'expert')), parts along dimension 0
- decoded: bfloat16 [4096, 1024], P(('groups', 'expert'), 'head'), parts along dimension 0
There are 2 independent parts, one for each index of `groups`. A program takes and returns all parts, laid end to end along the dimension named above; an argument that names none is the same for every part. Nothing has to cross between parts.
Inputs may be any that keep to these rules, and one draw needn't show every extreme that they name: `route_ids`: in each aligned block of 128 rows no expert is named more than 40 times, a bound that some block reaches. `src_lengths`: some sentence has exactly 64 live tokens. `tgt_lengths`: some sentence has exactly 64 live tokens.
All inputs are finite; a program needn't handle non-finite values.
Results may differ from a plain program's by a relative error of at most 0.025.
Values may be sent and summed in bfloat16 or wider, within the bound.
No kernel may reach another device: no remote copies, remote signals or barrier semaphores. Data moves between devices by JAX's collectives and lax.ppermute only.
A program may use at most 64 MiB of HBM per device.

v0:
```python
import jax
import jax.numpy as jnp
from jax import lax
from jax.sharding import PartitionSpec as P

DH = 64


def from_partner(x, axis, stride):
    return lax.ppermute(x, axis, [(i, i ^ 1 << stride) for i in range(lax.axis_size(axis))])


def layer_norm(rows, gain):
    rows = rows.astype(jnp.float32)
    mean = jnp.mean(rows, axis=-1, keepdims=True)
    centered = rows - mean
    spread = jnp.mean(centered * centered, axis=-1, keepdims=True)
    return centered * lax.rsqrt(spread + 1e-05) * gain


def partner(block):
    return from_partner(block, "expert", 0)


def shards(
    sources,
    enc_gain,
    route_ids,
    route_gates,
    w_in,
    w_out,
    targets,
    dec_gain,
    src_lengths,
    tgt_lengths,
    w_query,
    w_key,
    w_value,
    w_attn,
):
    tok_rows, width = sources.shape
    experts = lax.axis_size("expert") // 2
    capacity = 2 * ((5 * tok_rows + 4 * experts - 1) // (4 * experts))
    side = lax.axis_index("expert") % 2
    pair_ids = route_ids.reshape(-1)
    onehot = (pair_ids[:, None] == jnp.arange(experts, dtype=jnp.int32)[None, :]).astype(jnp.int32)
    earlier = jnp.cumsum(onehot, axis=0) - onehot
    slots = jnp.sum(earlier * onehot, axis=1)
    place = pair_ids * capacity + slots
    normed = layer_norm(sources, enc_gain).astype(jnp.bfloat16)
    outgoing = (
        jnp.zeros((experts * capacity, width), jnp.bfloat16)
        .at[place]
        .set(jnp.repeat(normed, 2, axis=0))
    )
    sending = outgoing.reshape(2 * experts, capacity // 2, width)
    arrived = lax.all_to_all(sending, "expert", split_axis=0, concat_axis=0, tiled=True)
    other = partner(arrived)
    lower = jnp.where(side == 0, arrived, other)
    upper = jnp.where(side == 0, other, arrived)
    arrived = jnp.concatenate((lower, upper), axis=1)
    expert_rows = arrived.reshape(-1, width)
    hidden = jnp.maximum(
        jnp.dot(expert_rows, w_in[0], preferred_element_type=jnp.float32), 0.0
    ).astype(jnp.bfloat16)
    quarter = jnp.dot(hidden, w_out[0], preferred_element_type=jnp.float32)
    half = lax.psum(quarter.astype(jnp.bfloat16), "head")
    kept = half.shape[1]
    half = half.reshape(2 * experts, capacity, kept)
    other_half = partner(half)
    merged = (half.astype(jnp.float32) + other_half.astype(jnp.float32)).astype(jnp.bfloat16)
    leaving = lax.dynamic_slice_in_dim(merged, side * (capacity // 2), capacity // 2, 1)
    returned = lax.all_to_all(leaving, "expert", split_axis=0, concat_axis=0, tiled=True)
    results = returned.reshape(-1, kept)
    picked = jnp.take(results, place, axis=0).astype(jnp.float32).reshape(tok_rows, 2, kept)
    moe = route_gates[:, 0:1] * picked[:, 0, :] + route_gates[:, 1:2] * picked[:, 1, :]
    memory = (sources.astype(jnp.float32) + moe).astype(jnp.bfloat16)
    w_q, w_k, w_v, w_o = (
        lax.all_gather(w_query, "expert", axis=0, tiled=True),
        lax.all_gather(w_key, "expert", axis=0, tiled=True),
        lax.all_gather(w_value, "expert", axis=0, tiled=True),
        lax.all_gather(w_attn, "expert", axis=0, tiled=True),
    )
    tnormed = layer_norm(targets, dec_gain).astype(jnp.bfloat16)
    query = jnp.dot(tnormed, w_q, preferred_element_type=jnp.float32).astype(jnp.bfloat16)
    key = jnp.dot(memory, w_k, preferred_element_type=jnp.float32).astype(jnp.bfloat16)
    value = jnp.dot(memory, w_v, preferred_element_type=jnp.float32).astype(jnp.bfloat16)
    sentences = src_lengths.shape[0]
    local_heads = query.shape[1] // DH
    queries = query.reshape(sentences, -1, local_heads, DH)
    keys = key.reshape(sentences, -1, local_heads, DH)
    values = value.reshape(sentences, -1, local_heads, DH)
    key_count = keys.shape[1]
    scores = jnp.einsum(
        "sqhd,skhd->shqk", queries, keys, preferred_element_type=jnp.float32
    ) * DH ** (-0.5)
    live = jnp.arange(key_count, dtype=jnp.int32)[None, :] < src_lengths[:, None]
    scores = jnp.where(live[:, None, None, :], scores, -1e30)
    top = jnp.max(scores, axis=-1, keepdims=True)
    raised = jnp.exp(scores - top)
    weights = (raised / jnp.sum(raised, axis=-1, keepdims=True)).astype(jnp.bfloat16)
    context = jnp.einsum(
        "shqk,skhd->sqhd", weights, values, preferred_element_type=jnp.float32
    ).astype(jnp.bfloat16)
    context = context.reshape(targets.shape[0], -1)
    partial_out = lax.dot_general(
        context, w_o, (((1,), (1,)), ((), ())), preferred_element_type=jnp.float32
    )
    attn = lax.psum_scatter(
        partial_out.astype(jnp.bfloat16), "head", scatter_dimension=1, tiled=True
    ).astype(jnp.float32)
    share = width // lax.axis_size("head")
    own_targets = lax.dynamic_slice_in_dim(
        targets, lax.axis_index("head") * share, share, 1
    ).astype(jnp.float32)
    per_sentence = targets.shape[0] // sentences
    positions = jnp.arange(targets.shape[0], dtype=jnp.int32)
    owner = positions // per_sentence
    live_rows = (positions % per_sentence < jnp.take(tgt_lengths, owner)).astype(jnp.float32)
    decoded = ((own_targets + attn) * live_rows[:, None]).astype(jnp.bfloat16)
    return (memory, decoded)


def solution(mesh):
    placed = (
        P(("groups", "expert"), None),
        P(),
        P(("groups", "expert"), None),
        P(("groups", "expert"), None),
        P("expert", None, "head"),
        P("expert", "head", None),
        P(("groups", "expert"), None),
        P(),
        P(("groups", "expert")),
        P(("groups", "expert")),
        P("expert", "head"),
        P("expert", "head"),
        P("expert", "head"),
        P("expert", "head"),
    )
    return jax.shard_map(
        shards,
        mesh=mesh,
        in_specs=placed,
        out_specs=(P(("groups", "expert"), None), P(("groups", "expert"), "head")),
        check_vma=False,
    )
```

profile of v0, /device:TPU:0, one launch (start us, length us, event | category | flops | bytes accessed | tf_op | source)
XLA Modules:
  0.0 201.6 jit_solution(6229918482698029241)
XLA Ops:
  7.2 0.7 all-gather.7.cloned.1.call-update
  7.9 0.7 all-gather.5.cloned.1.call-update
  8.6 0.8 copy.44
  9.7 0.7 broadcast_multiply_fusion
  10.7 0.6 reduce-window.6
  11.3 0.2 slice_reduce_fusion
  11.5 1.1 convert_reduce_fusion.1
  12.6 1.2 fusion.27
  13.8 1.2 fusion.29
  15.0 0.3 broadcast_in_dim.50
  15.2 0.2 reshape.235
  15.5 1.9 scatter_custom_fusion
  17.4 1.0 reshape.206
  18.5 7.4 %all-to-all-start = ((bf16[16,20,1024]{2,1,0:T(8,128)(2,1)}), bf16[16,20,1024]{2,1,0:T(8,128)(2,1)S(1)}, u32[]{:S(2)}, u32[]{:S(2)}) async-start(bf16[16,20,1024]{2,1,0:T(8,128)(2,1)} %reshape.206), calls=%async_computation | async-start | bytes 1572864 | tf_op jit(solution)/shard_map/all_to_all | solution.py:57
  25.9 0.7 all-gather.9.cloned.1.call-update
  26.6 19.0 %all-to-all-done = bf16[16,20,1024]{2,1,0:T(8,128)(2,1)S(1)} async-done(((bf16[16,20,1024]{2,1,0:T(8,128)(2,1)}), bf16[16,20,1024]{2,1,0:T(8,128)(2,1)S(1)}, u32[]{:S(2)}, u32[]{:S(2)}) %all-to-all-start) | async-done | bytes 655392 | tf_op jit(solution)/shard_map/all_to_all | solution.py:57
  45.6 0.4 copy.48
  46.0 0.3 collective-permute-start
  46.3 1.9 collective-permute-done
  48.2 0.4 broadcast_select_fusion.1
  48.6 0.3 pad_maximum_fusion
  48.9 9.1 %fusion.7 = bf16[640,1024]{1,0:T(8,128)(2,1)S(1)} fusion(bf16[1,2048,1024]{2,1,0:T(8,128)(2,1)} %param.19, bf16[640,1024]{1,0:T(8,128)(2,1)S(1)} %bitcast.61, bf16[1,1024,2048]{2,1,0:T(8,128)(2,1)} %param.18), kind=kOutput, calls=%fused_computation.8 | convolution fusion | flops 5371985920 | bytes 11010048 | tf_op jit(solution)/shard_map/dot_general | solution.py:66
  58.0 0.3 collective-permute-start.1
  58.4 0.6 fusion.55
  59.1 0.2 fusion.24
  59.4 1.8 collective-permute-done.1
  61.1 1.5 add_convert_fusion
  62.6 11.7 %all-to-all-start.1 = ((bf16[16,20,1024]{2,1,0:T(8,128)(2,1)}), bf16[16,20,1024]{2,1,0:T(8,128)(2,1)S(1)}, u32[]{:S(2)}, u32[]{:S(2)}) async-start(bf16[16,20,1024]{2,1,0:T(8,128)(2,1)} %add_convert_fusion), calls=%async_computation.1 | async-start | bytes 1572864 | tf_op jit(solution)/shard_map/all_to_all | solution.py:73
  74.3 1.3 compare_convert_fusion
  76.0 2.1 %convolution_convert_fusion.3 = bf16[128,1024]{1,0:T(8,128)(2,1)S(1)} fusion(bf16[1024,1024]{1,0:T(8,128)(2,1)} %all-gather.7.cloned.1.call-done, bf16[128,1024]{1,0:T(8,128)(2,1)S(1)} %copy-done, f32[1024]{0:T(1024)S(1)} %copy-done.4, f32[128]{0:T(128)S(1)} %add_rsqrt_fusion, f32[128]{0:T(128)S(1)} %broadcast_multiply_fusion.1), kind=kOutput, calls=%fused_computation.23 | convolution fusion | flops 269221888 | bytes 2626560 | tf_op jit(solution)/shard_map/dot_general | solution.py:85
  78.1 0.3 reshape.211
  78.5 15.5 %all-to-all-done.1 = bf16[16,20,1024]{2,1,0:T(8,128)(2,1)S(1)} async-done(((bf16[16,20,1024]{2,1,0:T(8,128)(2,1)}), bf16[16,20,1024]{2,1,0:T(8,128)(2,1)S(1)}, u32[]{:S(2)}, u32[]{:S(2)}) %all-to-all-start.1) | async-done | bytes 655392 | tf_op jit(solution)/shard_map/all_to_all | solution.py:73
  94.1 1.2 gather_fusion
  95.5 0.2 fusion.37
  95.8 0.5 copy-done.1
  96.4 10.8 %all-gather.5.cloned.1.call-done = bf16[1024,1024]{1,0:T(8,128)(2,1)} async-done(((bf16[64,1024]{1,0:T(8,128)(2,1)}), bf16[1024,1024]{1,0:T(8,128)(2,1)}) %all-gather.5.cloned.1.call-update) | async-done | bytes 2097168 | tf_op jit(solution)/shard_map/all_gather | solution.py:81
  107.3 2.0 %convolution_convert_fusion.4 = bf16[128,1024]{1,0:T(8,128)(2,1)S(1)} fusion(bf16[128,1024]{1,0:T(8,128)(2,1)S(1)} %fusion.30, bf16[1024,1024]{1,0:T(8,128)(2,1)} %all-gather.5.cloned.1.call-done), kind=kOutput, calls=%fused_computation.24 | convolution fusion | flops 268566528 | bytes 2621440 | tf_op jit(solution)/shard_map/dot_general | solution.py:87
  109.3 0.3 reshape.210
  109.7 40.1 %all-gather.9.cloned.1.call-done = bf16[1024,1024]{1,0:T(8,128)(2,1)} async-done(((bf16[64,1024]{1,0:T(8,128)(2,1)}), bf16[1024,1024]{1,0:T(8,128)(2,1)}) %all-gather.9.cloned.1.call-update) | async-done | bytes 2097168 | tf_op jit(solution)/shard_map/all_gather | solution.py:80
  149.8 2.0 %convolution_convert_fusion.2 = bf16[128,1024]{1,0:T(8,128)(2,1)S(1)} fusion(bf16[128,1024]{1,0:T(8,128)(2,1)S(1)} %fusion.30, bf16[1024,1024]{1,0:T(8,128)(2,1)} %all-gather.9.cloned.1.call-done), kind=kOutput, calls=%fused_computation.22 | convolution fusion | flops 268566528 | bytes 2621440 | tf_op jit(solution)/shard_map/dot_general | solution.py:86
  151.8 0.3 reshape.212
  152.2 0.6 fusion.56
  152.7 1.4 fusion.12
  154.1 2.0 %fusion.13 = bf16[2,64,16,64]{1,3,2,0:T(8,128)(2,1)S(1)} fusion(bf16[2,64,16,64]{3,2,1,0:T(8,128)(2,1)S(1)} %reshape.210, f32[2,16,64]{2,1,0:T(8,128)S(1)} %fusion.56, f32[2,16,64,64]{2,3,1,0:T(8,128)} %fusion.12), kind=kOutput, calls=%fused_computation.16 | convolution fusion | flops 17303616 | bytes 1056768 | tf_op jit(solution)/shard_map/shqk,skhd->sqhd/dot_general | solution.py:102
  156.2 0.4 copy.56
  156.6 0.3 reshape.213
  157.0 35.0 %all-gather.11.cloned.1.call-done = bf16[1024,1024]{1,0:T(8,128)(2,1)} async-done(((bf16[64,1024]{1,0:T(8,128)(2,1)}), bf16[1024,1024]{1,0:T(8,128)(2,1)}) %all-gather.11.cloned.1.call-update) | async-done | bytes 2097168 | tf_op jit(solution)/shard_map/all_gather | solution.py:82
  192.0 3.1 %fusion.17 = bf16[128,1024]{1,0:T(8,128)(2,1)} fusion(bf16[128,1024]{1,0:T(8,128)(2,1)S(1)} %reshape.213, bf16[1024,1024]{1,0:T(8,128)(2,1)} %all-gather.11.cloned.1.call-done, bf16[128,1024]{1,0:T(8,128)(2,1)S(1)} %copy-done, f32[128]{0:T(128)S(1)} %compare_convert_fusion), kind=kOutput, calls=%fused_computation.21 | convolution fusion | flops 269221888 | bytes 2884096 | tf_op jit(solution)/shard_map/dot_general | solution.py:106
  (44 shorter events, 1.8 us)
Async XLA Ops:
  7.2 68.9 %all-gather.7.cloned.1.call-start = ((), (), s32[]{:S(2)}) async-start(), calls=%async_computation.3 | async-start | bytes 2228224 | tf_op jit(solution)/shard_map/all_gather | solution.py:79
  7.9 99.4 %all-gather.5.cloned.1.call-start = ((), (), s32[]{:S(2)}) async-start(), calls=%async_computation.2 | async-start | bytes 2228224 | tf_op jit(solution)/shard_map/all_gather | solution.py:81
  18.5 27.2 %all-to-all-start = ((bf16[16,20,1024]{2,1,0:T(8,128)(2,1)}), bf16[16,20,1024]{2,1,0:T(8,128)(2,1)S(1)}, u32[]{:S(2)}, u32[]{:S(2)}) async-start(bf16[16,20,1024]{2,1,0:T(8,128)(2,1)} %reshape.206), calls=%async_computation | async-start | bytes 1572864 | tf_op jit(solution)/shard_map/all_to_all | solution.py:57
  25.8 123.9 %all-gather.9.cloned.1.call-start = ((), (), s32[]{:S(2)}) async-start(), calls=%async_computation.4 | async-start | bytes 2228224 | tf_op jit(solution)/shard_map/all_gather | solution.py:80
  26.6 165.4 %all-gather.11.cloned.1.call-start = ((), (), s32[]{:S(2)}) async-start(), calls=%async_computation.5 | async-start | bytes 2228224 | tf_op jit(solution)/shard_map/all_gather | solution.py:82
  46.0 2.2 %collective-permute-start = (bf16[16,20,1024]{2,0,1:T(8,128)(2,1)S(1)}, bf16[16,20,1024]{2,0,1:T(8,128)(2,1)S(1)}, u32[]{:S(2)}, u32[]{:S(2)}) collective-permute-start(bf16[16,20,1024]{2,0,1:T(8,128)(2,1)S(1)} %copy.48), channel_id=1, source_target_pairs={{0,1},{1,0},{2,3},{3,2},{4,5},{5,4},{6,7},{7,6},{8,9},{9,8},{10,11... | collective-permute-start | bytes 1966088 | tf_op jit(solution)/shard_map/ppermute | solution.py:10
  48.9 9.5 %copy-start.5 = (s32[2]{0:T(128)S(1)}, s32[2]{0:T(128)}, u32[]{:S(2)}) copy-start(s32[2]{0:T(128)} %param.23) | copy-start | bytes 28
  48.9 10.1 %copy-start = (bf16[128,1024]{1,0:T(8,128)(2,1)S(1)}, bf16[128,1024]{1,0:T(8,128)(2,1)}, u32[]{:S(2)}) copy-start(bf16[128,1024]{1,0:T(8,128)(2,1)} %param.20) | copy-start | bytes 786436
  58.0 3.1 %collective-permute-start.1 = (bf16[16,40,1024]{2,1,0:T(8,128)(2,1)S(1)}, bf16[16,40,1024]{2,1,0:T(8,128)(2,1)S(1)}, u32[]{:S(2)}, u32[]{:S(2)}) collective-permute-start(bf16[16,40,1024]{2,1,0:T(8,128)(2,1)S(1)} %bitcast.62), channel_id=1, source_target_pairs={{0,1},{1,0},{2,3},{3,2},{4,5},{5,4},{6,7},{7,6},{8,9},{9,8},{10,11... | collective-permute-start | bytes 3932168 | tf_op jit(solution)/shard_map/ppermute | solution.py:10
  59.3 16.6 %copy-start.7 = (s32[2]{0:T(128)S(1)}, s32[2]{0:T(128)}, u32[]{:S(2)}) copy-start(s32[2]{0:T(128)} %param.22) | copy-start | bytes 28
  59.3 16.6 %copy-start.6 = (f32[128,2]{0,1:T(2,128)S(1)}, f32[128,2]{0,1:T(2,128)}, u32[]{:S(2)}) copy-start(f32[128,2]{0,1:T(2,128)} %param.17) | copy-start | bytes 3076
  59.3 16.6 %copy-start.3 = (s32[128,2]{0,1:T(2,128)S(1)}, s32[128,2]{0,1:T(2,128)}, u32[]{:S(2)}) copy-start(s32[128,2]{0,1:T(2,128)} %param.16) | copy-start | bytes 3076
  59.3 16.7 %copy-start.4 = (f32[1024]{0:T(1024)S(1)}, f32[1024]{0:T(1024)}, u32[]{:S(2)}) copy-start(f32[1024]{0:T(1024)} %param.21) | copy-start | bytes 12292
  62.6 31.4 %all-to-all-start.1 = ((bf16[16,20,1024]{2,1,0:T(8,128)(2,1)}), bf16[16,20,1024]{2,1,0:T(8,128)(2,1)S(1)}, u32[]{:S(2)}, u32[]{:S(2)}) async-start(bf16[16,20,1024]{2,1,0:T(8,128)(2,1)} %add_convert_fusion), calls=%async_computation.1 | async-start | bytes 1572864 | tf_op jit(solution)/shard_map/all_to_all | solution.py:73
  95.3 1.0 copy-start.1
  96.4 55.4 %copy-start.2 = (bf16[128,1024]{1,0:T(8,128)(2,1)}, bf16[128,1024]{1,0:T(8,128)(2,1)S(1)}, u32[]{:S(2)}) copy-start(bf16[128,1024]{1,0:T(8,128)(2,1)S(1)} %fusion.30) | copy-start | bytes 786436
Sparse Core Ops, SparseCore 0:
  10.2 49.3 all-gather.6
  61.7 45.5 all-gather.4
  109.4 40.2 all-gather.8
  151.8 40.1 all-gather.10
where the time goes:
time: 202 us
  waiting for transfers between devices  126 us (62%)
  matrix products  22.4 us (11%)
  starting transfers between devices  19.8 us (10%)
  between operations  14.1 us (7%)
  local copies, waits for them, and re-layouts  9.9 us (5%)
  other arithmetic  9.17 us (5%)
    all_gather x1, waiting for transfers between devices, shards(): lax.all_gather(w_key, 'expert', axis=0, tiled=True)  40.1 us
    all_gather x1, waiting for transfers between devices, shards(): lax.all_gather(w_attn, 'expert', axis=0, tiled=True)  35 us
    all_to_all x1, waiting for transfers between devices, shards(): lax.all_to_all(sending, 'expert', split_axis=0, concat_axis=0, tiled=True)  19 us
    all_to_all x1, waiting for transfers between devices, shards(): lax.all_to_all(leaving, 'expert', split_axis=0, concat_axis=0, tiled=True)  15.5 us
    all_to_all x1, starting transfers between devices, shards(): lax.all_to_all(leaving, 'expert', split_axis=0, concat_axis=0, tiled=True)  11.7 us
    all_gather x1, waiting for transfers between devices, shards(): lax.all_gather(w_value, 'expert', axis=0, tiled=True)  10.8 us
    dot_general x1, matrix products, shards(): quarter = jnp.dot(hidden, w_out[0], preferred_element_type=jnp.float32)  9.11 us
    all_to_all x1, starting transfers between devices, shards(): lax.all_to_all(sending, 'expert', split_axis=0, concat_axis=0, tiled=True)  7.36 us
  transfers between devices with their start and end apart: 8, of which 7 were waited for; matrix products, arithmetic and copies ran while one was open for 19% of the time, Pallas kernels for 0%

commit v1 on v0

--- a/solution.py
+++ b/solution.py
@@ -4,6 +4,24 @@
 from jax.sharding import PartitionSpec as P
 
 DH = 64
+
+
+def collect(value, axis, dim):
+    ways, here, lap = (lax.axis_size(axis), lax.axis_index(axis), value.shape[dim])
+    shape = [n * ways if d == dim else n for d, n in enumerate(value.shape)]
+    full = lax.dynamic_update_slice_in_dim(
+        jnp.zeros(shape, value.dtype), value, here * lap, axis=dim
+    )
+    going_up = going_down = value
+    for far in range(1, ways // 2 + 1):
+        going_up = lax.ppermute(going_up, axis, [(d, (d + 1) % ways) for d in range(ways)])
+        full = lax.dynamic_update_slice_in_dim(full, going_up, (here - far) % ways * lap, axis=dim)
+        if 2 * far < ways:
+            going_down = lax.ppermute(going_down, axis, [(d, (d - 1) % ways) for d in range(ways)])
+            full = lax.dynamic_update_slice_in_dim(
+                full, going_down, (here + far) % ways * lap, axis=dim
+            )
+    return full
 
 
 def from_partner(x, axis, stride):
@@ -77,7 +95,7 @@
     memory = (sources.astype(jnp.float32) + moe).astype(jnp.bfloat16)
     w_q, w_k, w_v, w_o = (
         lax.all_gather(w_query, "expert", axis=0, tiled=True),
-        lax.all_gather(w_key, "expert", axis=0, tiled=True),
+        collect(w_key, "expert", 0),
         lax.all_gather(w_value, "expert", axis=0, tiled=True),
         lax.all_gather(w_attn, "expert", axis=0, tiled=True),
     )

time: 202 us -> 172 us (0.85)
  waiting for transfers between devices: 126 us -> 59.8 us
  starting transfers between devices: 19.8 us -> 51.5 us
  other arithmetic: 9.17 us -> 12.9 us
  local copies, waits for them, and re-layouts: 9.9 us -> 13.5 us
  matrix products: 22.4 us -> 19.5 us
    ppermute x0 -> x15, waiting for transfers between devices: none -> 42.1 us  [the longest x8 39.8 us: collect(): lax.ppermute(going_up, axis, [(d, (d + 1) % ways) for d in range(ways)])]
    all_gather x1 -> x0, waiting for transfers between devices: 40.1 us -> none  [shards(): lax.all_gather(w_key, 'expert', axis=0, tiled=True)]
    ppermute x0 -> x15, starting transfers between devices: none -> 35.9 us  [the longest x7 35 us: collect(): lax.ppermute(going_down, axis, [(d, (d - 1) % ways) for d in range(ways)])]
    all_gather x1, waiting for transfers between devices: 35 us -> 0.02 us  [shards(): lax.all_gather(w_attn, 'expert', axis=0, tiled=True)]
    all_to_all x1, waiting for transfers between devices: 15.5 us -> 0.01 us  [shards(): lax.all_to_all(leaving, 'expert', split_axis=0, concat_axis=0, tiled=True)]
    all_gather x1, waiting for transfers between devices: 10.8 us -> 0.02 us  [shards(): lax.all_gather(w_value, 'expert', axis=0, tiled=True)]
    all_to_all x1, starting transfers between devices: 11.7 us -> 4.42 us  [shards(): lax.all_to_all(leaving, 'expert', split_axis=0, concat_axis=0, tiled=True)]
    all_to_all x1, waiting for transfers between devices: 19 us -> 15.1 us  [shards(): lax.all_to_all(sending, 'expert', split_axis=0, concat_axis=0, tiled=True)]
  transfers between devices with their start and end apart: 8 -> 22, of which waited for: 7 -> 9; matrix products, arithmetic and copies ran while one was open for 19% -> 25% of each run, Pallas kernels for 0% -> 0%
where the time goes in v1:
time: 172 us; the launch traced here: 171 us
  waiting for transfers between devices  59.8 us (35%)
  starting transfers between devices  51.5 us (30%)
  matrix products  19.5 us (11%)
  between operations  14.2 us (8%)
  local copies, waits for them, and re-layouts  13.5 us (8%)
  other arithmetic  12.9 us (8%)
    ppermute x8, waiting for transfers between devices, collect(): lax.ppermute(going_up, axis, [(d, (d + 1) % ways) for d in range(ways)])  39.8 us
    ppermute x7, starting transfers between devices, collect(): lax.ppermute(going_down, axis, [(d, (d - 1) % ways) for d in range(ways)])  35 us
    all_to_all x1, waiting for transfers between devices, shards(): lax.all_to_all(sending, 'expert', split_axis=0, concat_axis=0, tiled=True)  15.1 us
    dot_general x1, matrix products, shards(): quarter = jnp.dot(hidden, w_out[0], preferred_element_type=jnp.float32)  10.2 us
    all_to_all x1, starting transfers between devices, shards(): lax.all_to_all(sending, 'expert', split_axis=0, concat_axis=0, tiled=True)  7.49 us
    all_to_all x1, starting transfers between devices, shards(): lax.all_to_all(leaving, 'expert', split_axis=0, concat_axis=0, tiled=True)  4.42 us
    ppermute x2, starting transfers between devices, from_partner(): lax.ppermute(x, axis, [(i, i ^ 1 << stride) for i in range(lax.axis_size(...  3.51 us
  transfers between devices with their start and end apart: 22, of which 9 were waited for; matrix products, arithmetic and copies ran while one was open for 25% of the time, Pallas kernels for 0%

profile of v1, /device:TPU:0, one launch (start us, length us, event | category | flops | bytes accessed | tf_op | source)
XLA Modules:
  0.0 171.3 jit_solution(11766893369650115447)
XLA Ops:
  7.2 0.7 all-gather.6.cloned.1.call-update
  7.9 0.7 all-gather.4.cloned.1.call-update
  8.6 0.8 copy.44
  9.7 0.7 broadcast_multiply_fusion
  10.7 0.6 reduce-window.6
  11.5 1.1 convert_reduce_fusion.1
  12.6 1.2 fusion.27
  13.8 1.2 fusion.29
  15.6 1.9 %scatter_custom_fusion = bf16[320,1024]{1,0:T(8,128)(2,1)S(1)} fusion(s32[256]{0:T(256)S(1)} %bitcast.63, bf16[256,1024]{1,0:T(8,128)(2,1)S(1)} %reshape.235, bf16[]{:T(256)} %constant.175.clone.1), kind=kCustom, calls=%fused_computation.55 | custom fusion | bytes 655362 | tf_op jit(solution)/shard_map/scatter | solution.py:72
  17.4 1.0 reshape.206
  18.5 7.5 %all-to-all-start = ((bf16[16,20,1024]{2,1,0:T(8,128)(2,1)}), bf16[16,20,1024]{2,1,0:T(8,128)(2,1)S(1)}, u32[]{:S(2)}, u32[]{:S(2)}) async-start(bf16[16,20,1024]{2,1,0:T(8,128)(2,1)} %reshape.206), calls=%async_computation | async-start | bytes 1572864 | tf_op jit(solution)/shard_map/all_to_all | solution.py:75
  26.0 0.5 collective-permute-start.2
  26.5 4.0 %collective-permute-start.3 = (bf16[64,1024]{1,0:T(8,128)(2,1)S(1)}, bf16[64,1024]{1,0:T(8,128)(2,1)S(1)}, u32[]{:S(2)}, u32[]{:S(2)}) collective-permute-start(bf16[64,1024]{1,0:T(8,128)(2,1)S(1)} %copy-done.5), channel_id=1, source_target_pairs={{0,15},{1,0},{2,1},{3,2},{4,3},{5,4},{6,5},{7,6},{8,7},{9,8},{10,9... | collective-permute-start | bytes 393224 | tf_op jit(solution)/shard_map/ppermute | solution.py:20
  30.9 15.1 %all-to-all-done = bf16[16,20,1024]{2,1,0:T(8,128)(2,1)S(1)} async-done(((bf16[16,20,1024]{2,1,0:T(8,128)(2,1)}), bf16[16,20,1024]{2,1,0:T(8,128)(2,1)S(1)}, u32[]{:S(2)}, u32[]{:S(2)}) %all-to-all-start) | async-done | bytes 655392 | tf_op jit(solution)/shard_map/all_to_all | solution.py:75
  46.4 3.1 %collective-permute-start = (bf16[16,20,1024]{2,0,1:T(8,128)(2,1)S(1)}, bf16[16,20,1024]{2,0,1:T(8,128)(2,1)S(1)}, u32[]{:S(2)}, u32[]{:S(2)}) collective-permute-start(bf16[16,20,1024]{2,0,1:T(8,128)(2,1)S(1)} %copy.48), channel_id=1, source_target_pairs={{0,1},{1,0},{2,3},{3,2},{4,5},{5,4},{6,7},{7,6},{8,9},{9,8},{10,11... | collective-permute-start | bytes 1966088 | tf_op jit(solution)/shard_map/ppermute | solution.py:28
  49.5 0.6 iota_compare_fusion.2
  50.1 1.1 collective-permute-done
  51.2 0.5 broadcast_select_fusion.1
  52.0 10.2 %fusion.7 = bf16[640,1024]{1,0:T(8,128)(2,1)} fusion(bf16[1,2048,1024]{2,1,0:T(8,128)(2,1)} %param.19, bf16[640,1024]{1,0:T(8,128)(2,1)S(1)} %bitcast.61, bf16[1,1024,2048]{2,1,0:T(8,128)(2,1)} %param.18), kind=kOutput, calls=%fused_computation.8 | convolution fusion | flops 5371985920 | bytes 11010048 | tf_op jit(solution)/shard_map/dot_general | solution.py:84
  62.9 0.6 fusion.55
  63.5 1.8 %compare_convert_fusion = f32[128]{0:T(128)} fusion(s32[]{:T(128)} %bitcast.14, s32[]{:T(128)} %bitcast.13), kind=kLoop, calls=%fused_computation.89 | loop fusion | flops 4352 | bytes 520 | tf_op jit(solution)/shard_map/convert_element_type | solution.py:137
  65.8 9.0 %collective-permute-start.5 = (bf16[64,1024]{1,0:T(8,128)(2,1)S(1)}, bf16[64,1024]{1,0:T(8,128)(2,1)S(1)}, u32[]{:S(2)}, u32[]{:S(2)}) collective-permute-start(bf16[64,1024]{1,0:T(8,128)(2,1)S(1)} %collective-permute-done.3), channel_id=1, source_target_pairs={{0,15},{1,0},{2,1},{3,2},{4,3},{5,4},{6,5},{7,6},{8,7},{9,8},{10,9... | collective-permute-start | bytes 393224 | tf_op jit(solution)/shard_map/ppermute | solution.py:20
  74.8 3.7 %collective-permute-done.4 = bf16[64,1024]{1,0:T(8,128)(2,1)S(1)} collective-permute-done((bf16[64,1024]{1,0:T(8,128)(2,1)S(1)}, bf16[64,1024]{1,0:T(8,128)(2,1)S(1)}, u32[]{:S(2)}, u32[]{:S(2)}) %collective-permute-start.4) | collective-permute-done | bytes 131104 | tf_op jit(solution)/shard_map/ppermute | solution.py:17
  78.6 4.4 %collective-permute-start.7 = (bf16[64,1024]{1,0:T(8,128)(2,1)S(1)}, bf16[64,1024]{1,0:T(8,128)(2,1)S(1)}, u32[]{:S(2)}, u32[]{:S(2)}) collective-permute-start(bf16[64,1024]{1,0:T(8,128)(2,1)S(1)} %collective-permute-done.5), channel_id=1, source_target_pairs={{0,15},{1,0},{2,1},{3,2},{4,3},{5,4},{6,5},{7,6},{8,7},{9,8},{10,9... | collective-permute-start | bytes 393224 | tf_op jit(solution)/shard_map/ppermute | solution.py:20
  83.0 2.7 %collective-permute-done.6 = bf16[64,1024]{1,0:T(8,128)(2,1)S(1)} collective-permute-done((bf16[64,1024]{1,0:T(8,128)(2,1)S(1)}, bf16[64,1024]{1,0:T(8,128)(2,1)S(1)}, u32[]{:S(2)}, u32[]{:S(2)}) %collective-permute-start.6) | collective-permute-done | bytes 131104 | tf_op jit(solution)/shard_map/ppermute | solution.py:17
  85.8 4.4 %collective-permute-start.9 = (bf16[64,1024]{1,0:T(8,128)(2,1)S(1)}, bf16[64,1024]{1,0:T(8,128)(2,1)S(1)}, u32[]{:S(2)}, u32[]{:S(2)}) collective-permute-start(bf16[64,1024]{1,0:T(8,128)(2,1)S(1)} %collective-permute-done.7), channel_id=1, source_target_pairs={{0,15},{1,0},{2,1},{3,2},{4,3},{5,4},{6,5},{7,6},{8,7},{9,8},{10,9... | collective-permute-start | bytes 393224 | tf_op jit(solution)/shard_map/ppermute | solution.py:20
  90.2 5.3 %collective-permute-done.8 = bf16[64,1024]{1,0:T(8,128)(2,1)S(1)} collective-permute-done((bf16[64,1024]{1,0:T(8,128)(2,1)S(1)}, bf16[64,1024]{1,0:T(8,128)(2,1)S(1)}, u32[]{:S(2)}, u32[]{:S(2)}) %collective-permute-start.8) | collective-permute-done | bytes 131104 | tf_op jit(solution)/shard_map/ppermute | solution.py:17
  95.5 4.4 %collective-permute-start.11 = (bf16[64,1024]{1,0:T(8,128)(2,1)S(1)}, bf16[64,1024]{1,0:T(8,128)(2,1)S(1)}, u32[]{:S(2)}, u32[]{:S(2)}) collective-permute-start(bf16[64,1024]{1,0:T(8,128)(2,1)S(1)} %collective-permute-done.9), channel_id=1, source_target_pairs={{0,15},{1,0},{2,1},{3,2},{4,3},{5,4},{6,5},{7,6},{8,7},{9,8},{10,9... | collective-permute-start | bytes 393224 | tf_op jit(solution)/shard_map/ppermute | solution.py:20
  99.9 3.0 %add_convert_fusion = bf16[16,20,1024]{2,1,0:T(8,128)(2,1)} fusion(bf16[16,40,1024]{2,1,0:T(8,128)(2,1)} %collective-permute-done.1, s32[]{:T(128)S(6)} %select_n.219, bf16[16,40,1024]{2,1,0:T(8,128)(2,1)} %bitcast.8), kind=kLoop, calls=%fused_computation.9 | loop fusion | flops 1310720 | bytes 1966084 | tf_op jit(solution)/shard_map/convert_element_type | solution.py:89
  103.0 4.4 %all-to-all-start.1 = ((bf16[16,20,1024]{2,1,0:T(8,128)(2,1)}), bf16[16,20,1024]{2,1,0:T(8,128)(2,1)}, u32[]{:S(2)}, u32[]{:S(2)}) async-start(bf16[16,20,1024]{2,1,0:T(8,128)(2,1)} %add_convert_fusion), calls=%async_computation.1 | async-start | bytes 1572864 | tf_op jit(solution)/shard_map/all_to_all | solution.py:91
  107.7 4.2 %collective-permute-start.13 = (bf16[64,1024]{1,0:T(8,128)(2,1)S(1)}, bf16[64,1024]{1,0:T(8,128)(2,1)S(1)}, u32[]{:S(2)}, u32[]{:S(2)}) collective-permute-start(bf16[64,1024]{1,0:T(8,128)(2,1)S(1)} %collective-permute-done.11), channel_id=1, source_target_pairs={{0,15},{1,0},{2,1},{3,2},{4,3},{5,4},{6,5},{7,6},{8,7},{9,8},{10,9... | collective-permute-start | bytes 393224 | tf_op jit(solution)/shard_map/ppermute | solution.py:20
  112.0 19.6 %collective-permute-done.12 = bf16[64,1024]{1,0:T(8,128)(2,1)S(1)} collective-permute-done((bf16[64,1024]{1,0:T(8,128)(2,1)S(1)}, bf16[64,1024]{1,0:T(8,128)(2,1)S(1)}, u32[]{:S(2)}, u32[]{:S(2)}) %collective-permute-start.12) | collective-permute-done | bytes 131104 | tf_op jit(solution)/shard_map/ppermute | solution.py:17
  131.6 4.4 %collective-permute-start.15 = (bf16[64,1024]{1,0:T(8,128)(2,1)S(1)}, bf16[64,1024]{1,0:T(8,128)(2,1)S(1)}, u32[]{:S(2)}, u32[]{:S(2)}) collective-permute-start(bf16[64,1024]{1,0:T(8,128)(2,1)S(1)} %collective-permute-done.13), channel_id=1, source_target_pairs={{0,15},{1,0},{2,1},{3,2},{4,3},{5,4},{6,5},{7,6},{8,7},{9,8},{10,9... | collective-permute-start | bytes 393224 | tf_op jit(solution)/shard_map/ppermute | solution.py:20
  136.1 2.6 %collective-permute-done.14 = bf16[64,1024]{1,0:T(8,128)(2,1)S(1)} collective-permute-done((bf16[64,1024]{1,0:T(8,128)(2,1)S(1)}, bf16[64,1024]{1,0:T(8,128)(2,1)S(1)}, u32[]{:S(2)}, u32[]{:S(2)}) %collective-permute-start.14) | collective-permute-done | bytes 131104 | tf_op jit(solution)/shard_map/ppermute | solution.py:17
  138.7 2.3 %collective-permute-done.15 = bf16[64,1024]{1,0:T(8,128)(2,1)S(1)} collective-permute-done((bf16[64,1024]{1,0:T(8,128)(2,1)S(1)}, bf16[64,1024]{1,0:T(8,128)(2,1)S(1)}, u32[]{:S(2)}, u32[]{:S(2)}) %collective-permute-start.15) | collective-permute-done | bytes 131104 | tf_op jit(solution)/shard_map/ppermute | solution.py:20
  141.0 5.9 %collective-permute-done.16 = bf16[64,1024]{1,0:T(8,128)(2,1)S(1)} collective-permute-done((bf16[64,1024]{1,0:T(8,128)(2,1)S(1)}, bf16[64,1024]{1,0:T(8,128)(2,1)S(1)}, u32[]{:S(2)}, u32[]{:S(2)}) %collective-permute-start.16) | collective-permute-done | bytes 131104 | tf_op jit(solution)/shard_map/ppermute | solution.py:17
  147.0 2.1 %convolution_convert_fusion.3 = bf16[128,1024]{1,0:T(8,128)(2,1)S(1)} fusion(bf16[1024,1024]{1,0:T(8,128)(2,1)} %all-gather.6.cloned.1.call-done, bf16[128,1024]{1,0:T(8,128)(2,1)S(1)} %copy-done, f32[1024]{0:T(1024)S(1)} %copy-done.7, f32[128]{0:T(128)S(1)} %add_rsqrt_fusion, f32[128]{0:T(128)S(1)} %broadcast_multiply_fusion.1), kind=kOutput, calls=%fused_computation.23 | convolution fusion | flops 269221888 | bytes 2626560 | tf_op jit(solution)/shard_map/dot_general | solution.py:103
  149.1 1.1 reshape.211
  150.2 1.2 reshape.209
  151.5 1.2 gather_fusion
  152.6 1.0 gather.11
  153.6 1.3 fusion.37
  155.1 2.1 %convolution_convert_fusion.4 = bf16[128,1024]{1,0:T(8,128)(2,1)S(1)} fusion(bf16[128,1024]{1,0:T(8,128)(2,1)S(1)} %fusion.30, bf16[1024,1024]{1,0:T(8,128)(2,1)} %all-gather.4.cloned.1.call-done), kind=kOutput, calls=%fused_computation.24 | convolution fusion | flops 268566528 | bytes 2621440 | tf_op jit(solution)/shard_map/dot_general | solution.py:105
  157.3 1.1 reshape.210
  158.4 0.4 convolution_convert_fusion.2
  159.2 0.6 fusion.56
  160.3 0.5 fusion.13
  161.6 3.1 %fusion.17 = bf16[128,1024]{1,0:T(8,128)(2,1)} fusion(bf16[128,1024]{1,0:T(8,128)(2,1)S(1)} %reshape.213, bf16[1024,1024]{1,0:T(8,128)(2,1)} %all-gather.8.cloned.1.call-done, bf16[128,1024]{1,0:T(8,128)(2,1)S(1)} %copy-done, f32[128]{0:T(128)S(1)} %copy-done.10), kind=kOutput, calls=%fused_computation.21 | convolution fusion | flops 269221888 | bytes 2884096 | tf_op jit(solution)/shard_map/dot_general | solution.py:124
  (98 shorter events, 6.0 us)
Async XLA Ops:
  7.2 139.8 %all-gather.6.cloned.1.call-start = ((), (), s32[]{:S(2)}) async-start(), calls=%async_computation.3 | async-start | bytes 2228224 | tf_op jit(solution)/shard_map/all_gather | solution.py:97
  7.9 147.2 %all-gather.4.cloned.1.call-start = ((), (), s32[]{:S(2)}) async-start(), calls=%async_computation.2 | async-start | bytes 2228224 | tf_op jit(solution)/shard_map/all_gather | solution.py:99
  15.4 10.6 %copy-start.5 = (bf16[64,1024]{1,0:T(8,128)(2,1)S(1)}, bf16[64,1024]{1,0:T(8,128)(2,1)}, u32[]{:S(2)}) copy-start(bf16[64,1024]{1,0:T(8,128)(2,1)} %param.25) | copy-start | bytes 393220
  15.5 15.1 %copy-start = (bf16[128,1024]{1,0:T(8,128)(2,1)S(1)}, bf16[128,1024]{1,0:T(8,128)(2,1)}, u32[]{:S(2)}) copy-start(bf16[128,1024]{1,0:T(8,128)(2,1)} %param.20) | copy-start | bytes 786436
  18.5 31.1 %copy-start.11 = (s32[2]{0:T(128)S(1)}, s32[2]{0:T(128)}, u32[]{:S(2)}) copy-start(s32[2]{0:T(128)} %param.22) | copy-start | bytes 28
  18.5 31.6 %copy-start.9 = (f32[128,2]{0,1:T(2,128)S(1)}, f32[128,2]{0,1:T(2,128)}, u32[]{:S(2)}) copy-start(f32[128,2]{0,1:T(2,128)} %param.17) | copy-start | bytes 3076
  18.5 27.6 %all-to-all-start = ((bf16[16,20,1024]{2,1,0:T(8,128)(2,1)}), bf16[16,20,1024]{2,1,0:T(8,128)(2,1)S(1)}, u32[]{:S(2)}, u32[]{:S(2)}) async-start(bf16[16,20,1024]{2,1,0:T(8,128)(2,1)} %reshape.206), calls=%async_computation | async-start | bytes 1572864 | tf_op jit(solution)/shard_map/all_to_all | solution.py:75
  26.0 135.6 %all-gather.8.cloned.1.call-start = ((), (), s32[]{:S(2)}) async-start(), calls=%async_computation.4 | async-start | bytes 2228224 | tf_op jit(solution)/shard_map/all_gather | solution.py:100
  26.0 39.6 %collective-permute-start.2 = (bf16[64,1024]{1,0:T(8,128)(2,1)S(1)}, bf16[64,1024]{1,0:T(8,128)(2,1)S(1)}, u32[]{:S(2)}, u32[]{:S(2)}) collective-permute-start(bf16[64,1024]{1,0:T(8,128)(2,1)S(1)} %copy-done.5), channel_id=1, source_target_pairs={{0,1},{1,2},{2,3},{3,4},{4,5},{5,6},{6,7},{7,8},{8,9},{9,10},{10,1... | collective-permute-start | bytes 393224 | tf_op jit(solution)/shard_map/ppermute | solution.py:17
  26.5 39.3 %collective-permute-start.3 = (bf16[64,1024]{1,0:T(8,128)(2,1)S(1)}, bf16[64,1024]{1,0:T(8,128)(2,1)S(1)}, u32[]{:S(2)}, u32[]{:S(2)}) collective-permute-start(bf16[64,1024]{1,0:T(8,128)(2,1)S(1)} %copy-done.5), channel_id=1, source_target_pairs={{0,15},{1,0},{2,1},{3,2},{4,3},{5,4},{6,5},{7,6},{8,7},{9,8},{10,9... | collective-permute-start | bytes 393224 | tf_op jit(solution)/shard_map/ppermute | solution.py:20
  46.4 4.8 %collective-permute-start = (bf16[16,20,1024]{2,0,1:T(8,128)(2,1)S(1)}, bf16[16,20,1024]{2,0,1:T(8,128)(2,1)S(1)}, u32[]{:S(2)}, u32[]{:S(2)}) collective-permute-start(bf16[16,20,1024]{2,0,1:T(8,128)(2,1)S(1)} %copy.48), channel_id=1, source_target_pairs={{0,1},{1,0},{2,3},{3,2},{4,5},{5,4},{6,7},{7,6},{8,9},{9,8},{10,11... | collective-permute-start | bytes 1966088 | tf_op jit(solution)/shard_map/ppermute | solution.py:28
  52.0 10.9 %copy-start.8 = (s32[2]{0:T(128)S(1)}, s32[2]{0:T(128)}, u32[]{:S(2)}) copy-start(s32[2]{0:T(128)} %param.23) | copy-start | bytes 28
  52.0 11.5 %copy-start.6 = (s32[128,2]{0,1:T(2,128)S(1)}, s32[128,2]{0,1:T(2,128)}, u32[]{:S(2)}) copy-start(s32[128,2]{0,1:T(2,128)} %param.16) | copy-start | bytes 3076
  62.3 37.7 %collective-permute-start.1 = (bf16[16,40,1024]{2,1,0:T(8,128)(2,1)}, bf16[16,40,1024]{2,1,0:T(8,128)(2,1)}, u32[]{:S(2)}, u32[]{:S(2)}) collective-permute-start(bf16[16,40,1024]{2,1,0:T(8,128)(2,1)} %bitcast.8), channel_id=1, source_target_pairs={{0,1},{1,0},{2,3},{3,2},{4,5},{5,4},{6,7},{7,6},{8,9},{9,8},{10,11... | collective-permute-start | bytes 3932168 | tf_op jit(solution)/shard_map/ppermute | solution.py:28
  65.6 12.9 %collective-permute-start.4 = (bf16[64,1024]{1,0:T(8,128)(2,1)S(1)}, bf16[64,1024]{1,0:T(8,128)(2,1)S(1)}, u32[]{:S(2)}, u32[]{:S(2)}) collective-permute-start(bf16[64,1024]{1,0:T(8,128)(2,1)S(1)} %collective-permute-done.2), channel_id=1, source_target_pairs={{0,1},{1,2},{2,3},{3,4},{4,5},{5,6},{6,7},{7,8},{8,9},{9,10},{10,1... | collective-permute-start | bytes 393224 | tf_op jit(solution)/shard_map/ppermute | solution.py:17
  65.8 12.8 %collective-permute-start.5 = (bf16[64,1024]{1,0:T(8,128)(2,1)S(1)}, bf16[64,1024]{1,0:T(8,128)(2,1)S(1)}, u32[]{:S(2)}, u32[]{:S(2)}) collective-permute-start(bf16[64,1024]{1,0:T(8,128)(2,1)S(1)} %collective-permute-done.3), channel_id=1, source_target_pairs={{0,15},{1,0},{2,1},{3,2},{4,3},{5,4},{6,5},{7,6},{8,7},{9,8},{10,9... | collective-permute-start | bytes 393224 | tf_op jit(solution)/shard_map/ppermute | solution.py:20
  78.5 7.2 %collective-permute-start.6 = (bf16[64,1024]{1,0:T(8,128)(2,1)S(1)}, bf16[64,1024]{1,0:T(8,128)(2,1)S(1)}, u32[]{:S(2)}, u32[]{:S(2)}) collective-permute-start(bf16[64,1024]{1,0:T(8,128)(2,1)S(1)} %collective-permute-done.4), channel_id=1, source_target_pairs={{0,1},{1,2},{2,3},{3,4},{4,5},{5,6},{6,7},{7,8},{8,9},{9,10},{10,1... | collective-permute-start | bytes 393224 | tf_op jit(solution)/shard_map/ppermute | solution.py:17
  78.6 7.2 %collective-permute-start.7 = (bf16[64,1024]{1,0:T(8,128)(2,1)S(1)}, bf16[64,1024]{1,0:T(8,128)(2,1)S(1)}, u32[]{:S(2)}, u32[]{:S(2)}) collective-permute-start(bf16[64,1024]{1,0:T(8,128)(2,1)S(1)} %collective-permute-done.5), channel_id=1, source_target_pairs={{0,15},{1,0},{2,1},{3,2},{4,3},{5,4},{6,5},{7,6},{8,7},{9,8},{10,9... | collective-permute-start | bytes 393224 | tf_op jit(solution)/shard_map/ppermute | solution.py:20
  85.7 9.7 %collective-permute-start.8 = (bf16[64,1024]{1,0:T(8,128)(2,1)S(1)}, bf16[64,1024]{1,0:T(8,128)(2,1)S(1)}, u32[]{:S(2)}, u32[]{:S(2)}) collective-permute-start(bf16[64,1024]{1,0:T(8,128)(2,1)S(1)} %collective-permute-done.6), channel_id=1, source_target_pairs={{0,1},{1,2},{2,3},{3,4},{4,5},{5,6},{6,7},{7,8},{8,9},{9,10},{10,1... | collective-permute-start | bytes 393224 | tf_op jit(solution)/shard_map/ppermute | solution.py:17
  85.8 9.7 %collective-permute-start.9 = (bf16[64,1024]{1,0:T(8,128)(2,1)S(1)}, bf16[64,1024]{1,0:T(8,128)(2,1)S(1)}, u32[]{:S(2)}, u32[]{:S(2)}) collective-permute-start(bf16[64,1024]{1,0:T(8,128)(2,1)S(1)} %collective-permute-done.7), channel_id=1, source_target_pairs={{0,15},{1,0},{2,1},{3,2},{4,3},{5,4},{6,5},{7,6},{8,7},{9,8},{10,9... | collective-permute-start | bytes 393224 | tf_op jit(solution)/shard_map/ppermute | solution.py:20
  95.5 12.0 %collective-permute-start.10 = (bf16[64,1024]{1,0:T(8,128)(2,1)S(1)}, bf16[64,1024]{1,0:T(8,128)(2,1)S(1)}, u32[]{:S(2)}, u32[]{:S(2)}) collective-permute-start(bf16[64,1024]{1,0:T(8,128)(2,1)S(1)} %collective-permute-done.8), channel_id=1, source_target_pairs={{0,1},{1,2},{2,3},{3,4},{4,5},{5,6},{6,7},{7,8},{8,9},{9,10},{10,1... | collective-permute-start | bytes 393224 | tf_op jit(solution)/shard_map/ppermute | solution.py:17
  95.5 12.2 %collective-permute-start.11 = (bf16[64,1024]{1,0:T(8,128)(2,1)S(1)}, bf16[64,1024]{1,0:T(8,128)(2,1)S(1)}, u32[]{:S(2)}, u32[]{:S(2)}) collective-permute-start(bf16[64,1024]{1,0:T(8,128)(2,1)S(1)} %collective-permute-done.9), channel_id=1, source_target_pairs={{0,15},{1,0},{2,1},{3,2},{4,3},{5,4},{6,5},{7,6},{8,7},{9,8},{10,9... | collective-permute-start | bytes 393224 | tf_op jit(solution)/shard_map/ppermute | solution.py:20
  103.0 44.0 %copy-start.7 = (f32[1024]{0:T(1024)S(1)}, f32[1024]{0:T(1024)}, u32[]{:S(2)}) copy-start(f32[1024]{0:T(1024)} %param.21) | copy-start | bytes 12292
  103.0 47.2 %all-to-all-start.1 = ((bf16[16,20,1024]{2,1,0:T(8,128)(2,1)}), bf16[16,20,1024]{2,1,0:T(8,128)(2,1)}, u32[]{:S(2)}, u32[]{:S(2)}) async-start(bf16[16,20,1024]{2,1,0:T(8,128)(2,1)} %add_convert_fusion), calls=%async_computation.1 | async-start | bytes 1572864 | tf_op jit(solution)/shard_map/all_to_all | solution.py:91
  107.5 24.1 %collective-permute-start.12 = (bf16[64,1024]{1,0:T(8,128)(2,1)S(1)}, bf16[64,1024]{1,0:T(8,128)(2,1)S(1)}, u32[]{:S(2)}, u32[]{:S(2)}) collective-permute-start(bf16[64,1024]{1,0:T(8,128)(2,1)S(1)} %collective-permute-done.10), channel_id=1, source_target_pairs={{0,1},{1,2},{2,3},{3,4},{4,5},{5,6},{6,7},{7,8},{8,9},{9,10},{10,1... | collective-permute-start | bytes 393224 | tf_op jit(solution)/shard_map/ppermute | solution.py:17
  107.7 23.8 %collective-permute-start.13 = (bf16[64,1024]{1,0:T(8,128)(2,1)S(1)}, bf16[64,1024]{1,0:T(8,128)(2,1)S(1)}, u32[]{:S(2)}, u32[]{:S(2)}) collective-permute-start(bf16[64,1024]{1,0:T(8,128)(2,1)S(1)} %collective-permute-done.11), channel_id=1, source_target_pairs={{0,15},{1,0},{2,1},{3,2},{4,3},{5,4},{6,5},{7,6},{8,7},{9,8},{10,9... | collective-permute-start | bytes 393224 | tf_op jit(solution)/shard_map/ppermute | solution.py:20
  131.6 7.1 %collective-permute-start.14 = (bf16[64,1024]{1,0:T(8,128)(2,1)S(1)}, bf16[64,1024]{1,0:T(8,128)(2,1)S(1)}, u32[]{:S(2)}, u32[]{:S(2)}) collective-permute-start(bf16[64,1024]{1,0:T(8,128)(2,1)S(1)} %collective-permute-done.12), channel_id=1, source_target_pairs={{0,1},{1,2},{2,3},{3,4},{4,5},{5,6},{6,7},{7,8},{8,9},{9,10},{10,1... | collective-permute-start | bytes 393224 | tf_op jit(solution)/shard_map/ppermute | solution.py:17
  131.6 9.4 %collective-permute-start.15 = (bf16[64,1024]{1,0:T(8,128)(2,1)S(1)}, bf16[64,1024]{1,0:T(8,128)(2,1)S(1)}, u32[]{:S(2)}, u32[]{:S(2)}) collective-permute-start(bf16[64,1024]{1,0:T(8,128)(2,1)S(1)} %collective-permute-done.13), channel_id=1, source_target_pairs={{0,15},{1,0},{2,1},{3,2},{4,3},{5,4},{6,5},{7,6},{8,7},{9,8},{10,9... | collective-permute-start | bytes 393224 | tf_op jit(solution)/shard_map/ppermute | solution.py:20
  138.7 8.2 %collective-permute-start.16 = (bf16[64,1024]{1,0:T(8,128)(2,1)S(1)}, bf16[64,1024]{1,0:T(8,128)(2,1)S(1)}, u32[]{:S(2)}, u32[]{:S(2)}) collective-permute-start(bf16[64,1024]{1,0:T(8,128)(2,1)S(1)} %collective-permute-done.14), channel_id=1, source_target_pairs={{0,1},{1,2},{2,3},{3,4},{4,5},{5,6},{6,7},{7,8},{8,9},{9,10},{10,1... | collective-permute-start | bytes 393224 | tf_op jit(solution)/shard_map/ppermute | solution.py:17
  152.6 2.3 %copy-start.1 = (bf16[128,1024]{1,0:T(8,128)(2,1)S(1)}, bf16[128,1024]{1,0:T(8,128)(2,1)}, u32[]{:S(2)}) copy-start(bf16[128,1024]{1,0:T(8,128)(2,1)} %param.14) | copy-start | bytes 786436
  155.1 3.8 %copy-start.2 = (bf16[128,1024]{1,0:T(8,128)(2,1)}, bf16[128,1024]{1,0:T(8,128)(2,1)S(1)}, u32[]{:S(2)}) copy-start(bf16[128,1024]{1,0:T(8,128)(2,1)S(1)} %fusion.30) | copy-start | bytes 786436
  157.2 2.0 %copy-start.3 = (bf16[2,64,16,64]{3,2,1,0:T(8,128)(2,1)S(1)}, bf16[2,64,16,64]{3,2,1,0:T(8,128)(2,1)}, u32[]{:S(2)}) copy-start(bf16[2,64,16,64]{3,2,1,0:T(8,128)(2,1)} %reshape.211) | copy-start | bytes 786436
  157.2 2.0 %copy-start.12 = (pred[2,64]{1,0:T(4,128)(4,1)S(1)}, pred[2,64]{1,0:T(4,128)(4,1)}, u32[]{:S(2)}) copy-start(pred[2,64]{1,0:T(4,128)(4,1)} %iota_compare_fusion.2) | copy-start | bytes 388
  159.2 1.0 copy-start.4
  160.3 1.3 copy-start.10
Sparse Core Ops, SparseCore 0:
  10.2 49.8 all-gather.5
  62.2 43.0 all-gather.3
  107.5 45.4 all-gather.7
